TPU v7x, 512 devices: a whole 4x8x8 slice. The times are simulated.
512 devices in a mesh: dom: 64 (over y, x, core), feat: 8 (over z).
Axes of the slice: x: 4, y: 8, z: 8, core: 2. Of those that a mesh axis runs over, the one named last changes fastest.
Arguments:
- features: bfloat16 [512, 196608], P('feat', 'dom'), may hold values from -16 to 16
- weights: bfloat16 [2, 512, 512], replicated, may hold values from -0.1875 to 0.1875
- tile_values: bfloat16 [4608, 128, 128], P('dom'), may hold values from 0 to 0.099609375
- tile_blocks: int32 [4608, 2], P('dom'), may hold values from 0 to 31
- tile_counts: int32 [64], P('dom'), may hold values from 36 to 72
- replica: int32 [64, 64, 16], P('dom'), may hold values from -1 to 3071, as said below
- cotangent: bfloat16 [512, 196608], P(None, ('dom', 'feat')), may hold values from -6 to 6
Outputs:
- output: bfloat16 [512, 196608], P(None, ('dom', 'feat'))
- feature_grad: bfloat16 [512, 196608], P('feat', 'dom')
- weight_grad: float32 [2, 512, 512], P(None, 'feat')
Inputs may be any that keep to these rules, and one draw needn't show every extreme that they name: `tile_blocks`: column 0 names a tile's source block and column 1 its destination block. replica[q, p, k] is the master slot on partition q of the vertex in mirror slot q * 16 + k of partition p, or -1 for an unused slot; the used slots of a pair (q, p) come first; no partition mirrors its own masters; each master partition fills all 16 slots toward at least one partition.
All inputs are finite; a program needn't handle non-finite values.
Results may differ from a plain program's by a relative error of at most 0.0058.
Values may be sent and summed in bfloat16 or wider, within the bound.
A program may use at most 64 MiB of HBM per device.

v0:
```python
import jax
import jax.numpy as jnp
from jax import lax
from jax.sharding import PartitionSpec as P


def gathered_total(x, axis):
    pieces = lax.all_gather(x, axis).astype(jnp.float32)
    return pieces.sum(axis=0)


def local(features, weights, tile_values, tile_blocks, tile_counts, replica, cotangent):
    feat_width, masters = features.shape
    tile_size = tile_values.shape[1]
    replica_rows = replica[0]
    slot_used = (replica_rows >= 0).reshape(-1)
    slot_index = jnp.where(replica_rows >= 0, replica_rows, 0).reshape(-1)
    tile_live = (jnp.arange(tile_values.shape[0]) < tile_counts[0]).astype(jnp.float32)
    source_blocks = tile_blocks[:, 0]
    target_blocks = tile_blocks[:, 1]

    def pull_mirrors(values_in):
        outgoing = jnp.where(
            slot_used[None, :],
            jnp.take(values_in, slot_index, axis=1),
            jnp.zeros((), values_in.dtype),
        )
        return lax.all_to_all(outgoing, "dom", split_axis=1, concat_axis=1, tiled=True)

    def push_mirrors(partial_value):
        incoming = lax.all_to_all(
            partial_value[:, masters:].astype(jnp.bfloat16),
            "dom",
            split_axis=1,
            concat_axis=1,
            tiled=True,
        ).astype(jnp.float32)
        targets = jnp.where(slot_used, slot_index, masters)
        return partial_value[:, :masters].at[:, targets].add(incoming, mode="drop")

    def spread(own_cols, forward):
        local_cols = jnp.concatenate([own_cols, pull_mirrors(own_cols)], 1)
        nblocks = local_cols.shape[1] // tile_size
        blocks = local_cols.reshape(feat_width, nblocks, tile_size)
        if forward:
            picked = jnp.take(blocks, source_blocks, axis=1)
            contrib = jnp.einsum(
                "fts,tsd->ftd", picked, tile_values, preferred_element_type=jnp.float32
            )
            segment = target_blocks
        else:
            picked = jnp.take(blocks, target_blocks, axis=1)
            contrib = jnp.einsum(
                "ftd,tsd->fts", picked, tile_values, preferred_element_type=jnp.float32
            )
            segment = source_blocks
        onehot = (segment[:, None] == jnp.arange(nblocks)[None, :]).astype(jnp.float32) * tile_live[
            :, None
        ]
        partial_value = jnp.einsum("ftd,tb->fbd", contrib, onehot, precision=lax.Precision.HIGHEST)
        return push_mirrors(partial_value.reshape(feat_width, nblocks * tile_size))

    aggregate = spread(features, True).astype(jnp.bfloat16)
    feat_rows, agg_rows = (
        lax.all_to_all(features, "feat", split_axis=1, concat_axis=0, tiled=True),
        lax.all_to_all(aggregate, "feat", split_axis=1, concat_axis=0, tiled=True),
    )
    preact = jnp.einsum("io,iv->ov", weights[0], feat_rows, preferred_element_type=jnp.float32)
    preact = preact + jnp.einsum(
        "io,iv->ov", weights[1], agg_rows, preferred_element_type=jnp.float32
    )
    sigmoid_z = jax.nn.sigmoid(preact)
    output = (preact * sigmoid_z).astype(jnp.bfloat16)
    slope = sigmoid_z * (1.0 + preact * (1.0 - sigmoid_z))
    pre_grad = (cotangent.astype(jnp.float32) * slope).astype(jnp.bfloat16)
    slice_start = lax.axis_index("feat") * feat_width
    grad_cols = lax.all_gather(pre_grad, "feat", axis=1, tiled=True)
    weight_slice = lax.dynamic_slice_in_dim(weights, slice_start, feat_width, 1)
    terms = jnp.stack(
        [
            jnp.einsum("iv,ov->io", features, grad_cols, preferred_element_type=jnp.float32),
            jnp.einsum("iv,ov->io", aggregate, grad_cols, preferred_element_type=jnp.float32),
        ]
    )
    weight_grad = gathered_total(terms.astype(jnp.bfloat16), "dom").astype(jnp.float32)
    back_slices = jnp.einsum(
        "kio,ov->kiv", weight_slice, grad_cols, preferred_element_type=jnp.float32
    ).astype(jnp.bfloat16)
    self_grad = back_slices[0]
    agg_grad = back_slices[1]
    back_terms = spread(agg_grad, False)
    feature_grad = (self_grad.astype(jnp.float32) + back_terms).astype(jnp.bfloat16)
    return (output, feature_grad, weight_grad)


def solution(mesh):
    return jax.shard_map(
        local,
        mesh=mesh,
        in_specs=(
            P("feat", "dom"),
            P(),
            P("dom", None, None),
            P("dom", None),
            P("dom"),
            P("dom", None, None),
            P(None, ("dom", "feat")),
        ),
        out_specs=(P(None, ("dom", "feat")), P("feat", "dom"), P(None, "feat", None)),
        check_vma=False,
    )
```

profile of v0, /device:TPU:1, one launch (start us, length us, event | category | flops | bytes accessed | tf_op | source)
XLA Modules:
  0.0 258.0 jit_solution(7112404868492813658)
XLA Ops:
  10.1 4.3 %gather_fusion = bf16[1024,64]{1,0:T(8,128)(2,1)} fusion(bf16[64,3072]{0,1:T(8,128)(2,1)S(1)} %copy.72, s32[1024]{0:T(1024)S(1)} %fusion.34), kind=kCustom, calls=%fused_computation.clone | custom fusion | bytes 266240 | tf_op jit(solution)/shard_map/jit(_take)/gather | solution.py:25
  16.6 11.6 %all-to-all-start.1 = ((bf16[64,2,512]{2,1,0:T(2,128)(2,1)}), bf16[64,2,512]{2,1,0:T(2,128)(2,1)S(1)}, u32[]{:S(2)}, u32[]{:S(2)}) async-start(bf16[64,2,512]{2,1,0:T(2,128)(2,1)} %reshape.201), calls=%async_computation.1 | async-start | bytes 262144 | tf_op jit(solution)/shard_map/all_to_all | solution.py:28
  30.8 8.6 %all-to-all-done.1 = bf16[64,2,512]{2,1,0:T(2,128)(2,1)S(1)} async-done(((bf16[64,2,512]{2,1,0:T(2,128)(2,1)}), bf16[64,2,512]{2,1,0:T(2,128)(2,1)S(1)}, u32[]{:S(2)}, u32[]{:S(2)}) %all-to-all-start.1) | async-done | bytes 131104 | tf_op jit(solution)/shard_map/all_to_all | solution.py:28
  39.9 1.8 gather_fusion.1
  41.7 2.1 convolution_bitcast_fusion.1
  43.8 2.7 %fusion.3 = f32[32,64,128]{2,0,1:T(8,128)S(1)} fusion(f32[64,72,128]{2,0,1:T(8,128)S(1)} %convolution_bitcast_fusion.1, f32[72]{0:T(128)S(1)} %compare_convert_fusion, s32[72]{0:T(128)S(1)} %get-tuple-element.29), kind=kOutput, calls=%fused_computation.11 | convolution fusion | flops 226497024 | bytes 3408448 | tf_op jit(solution)/shard_map/ftd,tb->fbd/dot_general | solution.py:60
  49.1 4.4 %all-to-all-start.2 = ((bf16[64,2,512]{2,1,0:T(2,128)(2,1)}), bf16[64,2,512]{2,1,0:T(2,128)(2,1)S(1)}, u32[]{:S(2)}, u32[]{:S(2)}) async-start(bf16[64,2,512]{2,1,0:T(2,128)(2,1)} %reshape.203), calls=%async_computation.2 | async-start | bytes 262144 | tf_op jit(solution)/shard_map/all_to_all | solution.py:31
  54.3 10.6 %all-to-all-done.2 = bf16[64,2,512]{2,1,0:T(2,128)(2,1)S(1)} async-done(((bf16[64,2,512]{2,1,0:T(2,128)(2,1)}), bf16[64,2,512]{2,1,0:T(2,128)(2,1)S(1)}, u32[]{:S(2)}, u32[]{:S(2)}) %all-to-all-start.2) | async-done | bytes 131104 | tf_op jit(solution)/shard_map/all_to_all | solution.py:31
  64.9 10.0 %all-to-all-start = ((bf16[64,8,384]{2,0,1:T(8,128)(2,1)}), bf16[64,8,384]{2,0,1:T(8,128)(2,1)}, u32[]{:S(2)}, u32[]{:S(2)}) async-start(bf16[64,8,384]{2,0,1:T(8,128)(2,1)} %bitcast.122), calls=%async_computation | async-start | bytes 786432 | tf_op jit(solution)/shard_map/all_to_all | solution.py:65
  76.8 1.6 copy.78
  79.6 8.2 %scatter_custom_fusion = f32[64,3072]{0,1:T(8,128)} fusion(f32[64,3072]{0,1:T(8,128)} %copy.78, s32[1024]{0:T(1024)} %bitcast.140, bf16[64,1024]{0,1:T(8,128)(2,1)S(1)} %bitcast.133), kind=kCustom, calls=%fused_computation.42 | custom fusion | flops 131072 | bytes 917504 | tf_op jit(solution)/shard_map/scatter-add | solution.py:39
  87.8 1.5 convert_element_type.61
  90.3 6.6 %all-to-all-start.3 = ((bf16[64,8,384]{2,0,1:T(8,128)(2,1)}), bf16[64,8,384]{2,0,1:T(8,128)(2,1)}, u32[]{:S(2)}, u32[]{:S(2)}) async-start(bf16[64,8,384]{2,0,1:T(8,128)(2,1)} %copy.79), calls=%async_computation.3 | async-start | bytes 786432 | tf_op jit(solution)/shard_map/all_to_all | solution.py:66
  97.2 2.5 fusion.19
  99.7 10.8 %all-to-all-done.3 = bf16[64,8,384]{2,0,1:T(8,128)(2,1)} async-done(((bf16[64,8,384]{2,0,1:T(8,128)(2,1)}), bf16[64,8,384]{2,0,1:T(8,128)(2,1)}, u32[]{:S(2)}, u32[]{:S(2)}) %all-to-all-start.3) | async-done | bytes 393248 | tf_op jit(solution)/shard_map/all_to_all | solution.py:66
  110.4 3.1 %multiply_convert_fusion = (bf16[512,384]{1,0:T(8,128)(2,1)}, bf16[512,384]{1,0:T(8,128)(2,1)}) fusion(bf16[512,384]{1,0:T(8,128)(2,1)} %param.17, f32[512,384]{1,0:T(8,128)} %fusion.19, bf16[512,384]{1,0:T(8,128)(2,1)} %bitcast.19, bf16[2,512,512]{2,1,0:T(8,128)(2,1)} %param.12), kind=kOutput, calls=%fused_computation.30 | convolution fusion | flops 203882496 | bytes 2883584 | tf_op jit(solution)/shard_map/io,iv->ov/dot_general | solution.py:69
  113.6 38.6 %all-gather.3.cloned.1.call-done = bf16[512,3072]{1,0:T(8,128)(2,1)} async-done(((bf16[512,384]{1,0:T(8,128)(2,1)}), bf16[512,3072]{1,0:T(8,128)(2,1)}) %all-gather.3.cloned.1.call-update) | async-done | bytes 3145744 | tf_op jit(solution)/shard_map/all_gather | solution.py:77
  152.2 3.1 %fusion.13 = bf16[1,1,64,512]{3,2,1,0:T(8,128)(2,1)S(1)} fusion(bf16[64,3072]{0,1:T(8,128)(2,1)S(1)} %convert_element_type.61, bf16[512,3072]{1,0:T(8,128)(2,1)} %all-gather.3.cloned.1.call-done), kind=kOutput, calls=%fused_computation.26 | convolution fusion | flops 201359360 | bytes 3604480 | tf_op jit(solution)/shard_map/iv,ov->io/dot_general | solution.py:82
  157.1 2.6 convolution_convert_fusion
  161.0 4.3 %gather_fusion.2 = bf16[1024,64]{1,0:T(8,128)(2,1)} fusion(bf16[64,3072]{0,1:T(8,128)(2,1)S(1)} %copy.81, s32[1024]{0:T(1024)S(1)} %fusion.34), kind=kCustom, calls=%fused_computation.2.clone | custom fusion | bytes 266240 | tf_op jit(solution)/shard_map/jit(_take)/gather | solution.py:25
  166.8 22.9 %all_to_all.80 = bf16[64,2,512]{2,1,0:T(2,128)(2,1)S(1)} all-to-all(bf16[64,2,512]{2,1,0:T(2,128)(2,1)S(1)} %reshape.205), channel_id=1, replica_groups=mesh['dom'=64,'feat'=8] {'dom'}, dimensions={0} | all-to-all | bytes 262144 | tf_op jit(solution)/shard_map/all_to_all | solution.py:28
  190.2 1.9 gather_fusion.3
  192.1 3.0 %convolution_bitcast_fusion = f32[64,72,128]{2,0,1:T(8,128)S(1)} fusion(bf16[72,128,128]{2,1,0:T(8,128)(2,1)S(1)} %copy-done, bf16[72,64,128]{2,1,0:T(8,128)(2,1)} %gather_fusion.3, pred[72]{0:T(512)(128)(4,1)S(1)} %copy-done.11), kind=kOutput, calls=%fused_computation.13 | convolution fusion | flops 151584768 | bytes 5898312 | tf_op jit(solution)/shard_map/ftd,tsd->fts/dot_general | solution.py:53
  195.1 2.7 %fusion.1 = f32[32,64,128]{2,0,1:T(8,128)S(1)} fusion(f32[64,72,128]{2,0,1:T(8,128)S(1)} %convolution_bitcast_fusion, s32[72]{0:T(128)S(1)} %copy-done.12, f32[72]{0:T(128)S(1)} %copy-done.10), kind=kOutput, calls=%fused_computation.9 | convolution fusion | flops 226497024 | bytes 3408448 | tf_op jit(solution)/shard_map/ftd,tb->fbd/dot_general | solution.py:60
  199.3 1.8 reshape.207
  201.0 4.5 %all-to-all-start.5 = ((bf16[64,2,512]{2,1,0:T(2,128)(2,1)}), bf16[64,2,512]{2,1,0:T(2,128)(2,1)S(1)}, u32[]{:S(2)}, u32[]{:S(2)}) async-start(bf16[64,2,512]{2,1,0:T(2,128)(2,1)} %reshape.207), calls=%async_computation.5 | async-start | bytes 262144 | tf_op jit(solution)/shard_map/all_to_all | solution.py:31
  205.5 1.9 slice_add_fusion
  207.5 2.8 %copy.86 = f32[64,3072]{0,1:T(8,128)} copy(f32[64,3072]{1,0:T(8,128)} %slice_add_fusion) | data formatting | bytes 1572864 | tf_op jit(solution)/shard_map/add
  210.3 6.6 %all-to-all-done.5 = bf16[64,2,512]{2,1,0:T(2,128)(2,1)S(1)} async-done(((bf16[64,2,512]{2,1,0:T(2,128)(2,1)}), bf16[64,2,512]{2,1,0:T(2,128)(2,1)S(1)}, u32[]{:S(2)}, u32[]{:S(2)}) %all-to-all-start.5) | async-done | bytes 131104 | tf_op jit(solution)/shard_map/all_to_all | solution.py:31
  217.1 8.2 %scatter_custom_fusion.1 = f32[64,3072]{0,1:T(8,128)} fusion(f32[64,3072]{0,1:T(8,128)} %copy.86, s32[1024]{0:T(1024)} %bitcast.141, bf16[64,1024]{0,1:T(8,128)(2,1)S(1)} %bitcast.132), kind=kCustom, calls=%fused_computation.40 | custom fusion | flops 131072 | bytes 917504 | tf_op jit(solution)/shard_map/scatter-add | solution.py:39
  227.8 17.9 %all-gather.5.cloned.1.call-done = bf16[64,2,64,512]{3,2,1,0:T(8,128)(2,1)} async-done(((bf16[1,2,64,512]{3,2,1,0:T(8,128)(2,1)}), bf16[64,2,64,512]{3,2,1,0:T(8,128)(2,1)}) %all-gather.5.cloned.1.call-update) | async-done | bytes 8388624 | tf_op jit(solution)/shard_map/all_gather | solution.py:8
  245.7 5.5 %convert_reduce_fusion = f32[2,64,512]{2,1,0:T(8,128)} fusion(bf16[64,2,64,512]{3,2,1,0:T(8,128)(2,1)} %all-gather.5.cloned.1.call-done), kind=kLoop, calls=%fused_computation.6 | loop fusion | flops 8323072 | bytes 8650752 | tf_op jit(solution)/shard_map/reduce_sum | solution.py:9
  (70 shorter events, 24.3 us)
Async XLA Ops:
  7.2 34.5 %copy-start = (bf16[72,128,128]{2,1,0:T(8,128)(2,1)S(1)}, bf16[72,128,128]{2,1,0:T(8,128)(2,1)}, u32[]{:S(2)}) copy-start(bf16[72,128,128]{2,1,0:T(8,128)(2,1)} %param.13) | copy-start | bytes 7077892
  7.2 32.5 %copy-start.2 = (bf16[64,3072]{1,0:T(8,128)(2,1)S(1)}, bf16[64,3072]{1,0:T(8,128)(2,1)}, u32[]{:S(2)}) copy-start(bf16[64,3072]{1,0:T(8,128)(2,1)} %param.11) | copy-start | bytes 1179652
  7.2 21.0 %copy-start.8 = (s32[72,2]{0,1:T(2,128)S(1)}, s32[72,2]{0,1:T(2,128)}, u32[]{:S(2)}) copy-start(s32[72,2]{0,1:T(2,128)} %param.14) | copy-start | bytes 1732
  8.1 0.6 copy-start.6
  16.6 22.7 %all-to-all-start.1 = ((bf16[64,2,512]{2,1,0:T(2,128)(2,1)}), bf16[64,2,512]{2,1,0:T(2,128)(2,1)S(1)}, u32[]{:S(2)}, u32[]{:S(2)}) async-start(bf16[64,2,512]{2,1,0:T(2,128)(2,1)} %reshape.201), calls=%async_computation.1 | async-start | bytes 262144 | tf_op jit(solution)/shard_map/all_to_all | solution.py:28
  29.5 14.3 %copy-start.9 = (f32[72]{0:T(128)}, f32[72]{0:T(128)S(1)}, u32[]{:S(2)}) copy-start(f32[72]{0:T(128)S(1)} %compare_convert_fusion) | copy-start | bytes 868
  46.4 28.5 %copy-start.7 = (s32[1,64,16]{2,1,0:T(8,128)S(1)}, s32[1,64,16]{2,1,0:T(8,128)}, u32[]{:S(2)}) copy-start(s32[1,64,16]{2,1,0:T(8,128)} %copy-done.6) | copy-start | bytes 12292
  47.1 1.0 copy-start.3
  49.1 15.8 %all-to-all-start.2 = ((bf16[64,2,512]{2,1,0:T(2,128)(2,1)}), bf16[64,2,512]{2,1,0:T(2,128)(2,1)S(1)}, u32[]{:S(2)}, u32[]{:S(2)}) async-start(bf16[64,2,512]{2,1,0:T(2,128)(2,1)} %reshape.203), calls=%async_computation.2 | async-start | bytes 262144 | tf_op jit(solution)/shard_map/all_to_all | solution.py:31
  64.9 10.1 %copy-start.5 = (bf16[64,2,512]{2,1,0:T(2,128)(2,1)}, bf16[64,2,512]{2,1,0:T(2,128)(2,1)S(1)}, u32[]{:S(2)}) copy-start(bf16[64,2,512]{2,1,0:T(2,128)(2,1)S(1)} %all-to-all-done.2) | copy-start | bytes 393220
  64.9 25.4 %all-to-all-start = ((bf16[64,8,384]{2,0,1:T(8,128)(2,1)}), bf16[64,8,384]{2,0,1:T(8,128)(2,1)}, u32[]{:S(2)}, u32[]{:S(2)}) async-start(bf16[64,8,384]{2,0,1:T(8,128)(2,1)} %bitcast.122), calls=%async_computation | async-start | bytes 786432 | tf_op jit(solution)/shard_map/all_to_all | solution.py:65
  90.3 20.1 %all-to-all-start.3 = ((bf16[64,8,384]{2,0,1:T(8,128)(2,1)}), bf16[64,8,384]{2,0,1:T(8,128)(2,1)}, u32[]{:S(2)}, u32[]{:S(2)}) async-start(bf16[64,8,384]{2,0,1:T(8,128)(2,1)} %copy.79), calls=%async_computation.3 | async-start | bytes 786432 | tf_op jit(solution)/shard_map/all_to_all | solution.py:66
  96.9 55.3 %all-gather.3.cloned.1.call-start = ((), (), s32[]{:S(2)}) async-start(), calls=%async_computation.6 | async-start | bytes 3538944 | tf_op jit(solution)/shard_map/all_gather | solution.py:77
  113.6 132.1 %all-gather.5.cloned.1.call-start = ((), (), s32[]{:S(2)}) async-start(), calls=%async_computation.7 | async-start | bytes 8519680 | tf_op jit(solution)/shard_map/all_gather | solution.py:8
  152.2 3.1 %copy-start.1 = (bf16[512,3072]{1,0:T(8,128)(2,1)S(1)}, bf16[512,3072]{1,0:T(8,128)(2,1)}, u32[]{:S(2)}) copy-start(bf16[512,3072]{1,0:T(8,128)(2,1)} %all-gather.3.cloned.1.call-done) | copy-start | bytes 9437188
  159.6 0.9 copy-start.4
  166.6 25.5 %copy-start.11 = (pred[72]{0:T(512)(128)(4,1)S(1)}, pred[72]{0:T(512)(128)(4,1)}, u32[]{:S(2)}) copy-start(pred[72]{0:T(512)(128)(4,1)} %get-tuple-element.20) | copy-start | bytes 220
  192.1 3.0 %copy-start.10 = (f32[72]{0:T(128)S(1)}, f32[72]{0:T(128)}, u32[]{:S(2)}) copy-start(f32[72]{0:T(128)} %copy-done.9) | copy-start | bytes 868
  192.1 3.0 %copy-start.12 = (s32[72]{0:T(128)S(1)}, s32[72]{0:T(128)}, u32[]{:S(2)}) copy-start(s32[72]{0:T(128)} %get-tuple-element.28) | copy-start | bytes 868
  201.0 15.8 %all-to-all-start.5 = ((bf16[64,2,512]{2,1,0:T(2,128)(2,1)}), bf16[64,2,512]{2,1,0:T(2,128)(2,1)S(1)}, u32[]{:S(2)}, u32[]{:S(2)}) async-start(bf16[64,2,512]{2,1,0:T(2,128)(2,1)} %reshape.207), calls=%async_computation.5 | async-start | bytes 262144 | tf_op jit(solution)/shard_map/all_to_all | solution.py:31
Sparse Core Ops, SparseCore 0:
  113.7 38.4 all-gather.2
  157.2 88.4 all-gather.4
where the time goes:
time: 259 us; the launch traced here: 258 us
  waiting for transfers between devices  92.9 us (36%)
  starting transfers between devices  37.5 us (14%)
  local copies, waits for them, and re-layouts  35.4 us (14%)
  other arithmetic  31.5 us (12%)
  blocking collectives  22.9 us (9%)
  matrix products  22.7 us (9%)
  between operations  15 us (6%)
    all_gather x1, waiting for transfers between devices, local(): grad_cols = lax.all_gather(pre_grad, 'feat', axis=1, tiled=True)  38.6 us
    all_to_all x1, blocking collectives, pull_mirrors(): lax.all_to_all(outgoing, 'dom', split_axis=1, concat_axis=1, tiled=True)  22.9 us
    all_gather x1, waiting for transfers between devices, gathered_total(): pieces = lax.all_gather(x, axis).astype(jnp.float32)  17.9 us
    all_to_all x2, waiting for transfers between devices, push_mirrors(): lax.all_to_all(partial_value[:, masters:].astype(jnp.bfloat16), 'dom', sp...  17.1 us
    scatter-add x2, other arithmetic, push_mirrors(): return partial_value[:, :masters].at[:, targets].add(incoming, mode='drop')  16.4 us
    unnamed x39, local copies, waits for them, and re-layouts  12.5 us
    all_to_all x1, starting transfers between devices, pull_mirrors(): lax.all_to_all(outgoing, 'dom', split_axis=1, concat_axis=1, tiled=True)  11.6 us
    all_to_all x1, waiting for transfers between devices, local(): lax.all_to_all(aggregate, 'feat', split_axis=1, concat_axis=0, tiled=True)  10.8 us
  transfers between devices with their start and end apart: 7, of which 6 were waited for; matrix products, arithmetic and copies ran while one was open for 22% of the time, Pallas kernels for 0%

commit v1 on v0

--- a/solution.py
+++ b/solution.py
@@ -74,7 +74,9 @@
     slope = sigmoid_z * (1.0 + preact * (1.0 - sigmoid_z))
     pre_grad = (cotangent.astype(jnp.float32) * slope).astype(jnp.bfloat16)
     slice_start = lax.axis_index("feat") * feat_width
-    grad_cols = lax.all_gather(pre_grad, "feat", axis=1, tiled=True)
+    grad_cols = jnp.concatenate(
+        lax.all_to_all(jnp.stack([pre_grad] * lax.axis_size("feat")), "feat", 0, 0), axis=1
+    )
     weight_slice = lax.dynamic_slice_in_dim(weights, slice_start, feat_width, 1)
     terms = jnp.stack(
         [

time: 259 us -> 289 us (1.12)
  blocking collectives: 22.9 us -> 91.5 us
  waiting for transfers between devices: 92.9 us -> 42.8 us
  local copies, waits for them, and re-layouts: 35.4 us -> 48.7 us
    all_to_all x0 -> x1, blocking collectives: none -> 73.1 us  [local(): lax.all_to_all(jnp.stack([pre_grad] * lax.axis_size('feat')), 'feat', 0, 0)]
    all_gather x1 -> x0, waiting for transfers between devices: 38.6 us -> none  [local(): grad_cols = lax.all_gather(pre_grad, 'feat', axis=1, tiled=True)]
    all_gather x1, waiting for transfers between devices: 17.9 us -> 5.5 us  [gathered_total(): pieces = lax.all_gather(x, axis).astype(jnp.float32)]
    reshape x0 -> x3, local copies, waits for them, and re-layouts: none -> 11.9 us  [local(): jnp.concatenate(lax.all_to_all(jnp.stack([pre_grad] * lax.axis_size('feat...]
    all_to_all x1, blocking collectives: 22.9 us -> 18.4 us  [pull_mirrors(): lax.all_to_all(outgoing, 'dom', split_axis=1, concat_axis=1, tiled=True)]
  transfers between devices with their start and end apart: 7 -> 6, of which waited for: 6 -> 5; matrix products, arithmetic and copies ran while one was open for 22% -> 23% of each run, Pallas kernels for 0% -> 0%
where the time goes in v1:
time: 289 us; the launch traced here: 288 us
  blocking collectives  91.5 us (32%)
  local copies, waits for them, and re-layouts  48.7 us (17%)
  waiting for transfers between devices  42.8 us (15%)
  starting transfers between devices  37.4 us (13%)
  other arithmetic  31.5 us (11%)
  matrix products  20.6 us (7%)
  between operations  15 us (5%)
    all_to_all x1, blocking collectives, local(): lax.all_to_all(jnp.stack([pre_grad] * lax.axis_size('feat')), 'feat', 0, 0)  73.1 us
    all_to_all x1, blocking collectives, pull_mirrors(): lax.all_to_all(outgoing, 'dom', split_axis=1, concat_axis=1, tiled=True)  18.4 us
    all_to_all x2, waiting for transfers between devices, push_mirrors(): lax.all_to_all(partial_value[:, masters:].astype(jnp.bfloat16), 'dom', sp...  18 us
    scatter-add x2, other arithmetic, push_mirrors(): return partial_value[:, :masters].at[:, targets].add(incoming, mode='drop')  16.4 us
    unnamed x39, local copies, waits for them, and re-layouts  13.5 us
    reshape x3, local copies, waits for them, and re-layouts, local(): jnp.concatenate(lax.all_to_all(jnp.stack([pre_grad] * lax.axis_size('feat...  11.9 us
    all_to_all x1, starting transfers between devices, pull_mirrors(): lax.all_to_all(outgoing, 'dom', split_axis=1, concat_axis=1, tiled=True)  11.6 us
    all_to_all x1, waiting for transfers between devices, local(): lax.all_to_all(aggregate, 'feat', split_axis=1, concat_axis=0, tiled=True)  10.7 us
  transfers between devices with their start and end apart: 6, of which 5 were waited for; matrix products, arithmetic and copies ran while one was open for 23% of the time, Pallas kernels for 0%

profile of v1, /device:TPU:1, one launch (start us, length us, event | category | flops | bytes accessed | tf_op | source)
XLA Modules:
  0.0 287.5 jit_solution(14868256337455290238)
XLA Ops:
  10.1 4.3 %gather_fusion = bf16[1024,64]{1,0:T(8,128)(2,1)} fusion(bf16[64,3072]{0,1:T(8,128)(2,1)S(1)} %copy.73, s32[1024]{0:T(1024)S(1)} %fusion.33), kind=kCustom, calls=%fused_computation.clone | custom fusion | bytes 266240 | tf_op jit(solution)/shard_map/jit(_take)/gather | solution.py:25
  16.6 11.6 %all-to-all-start.1 = ((bf16[64,2,512]{2,1,0:T(2,128)(2,1)}), bf16[64,2,512]{2,1,0:T(2,128)(2,1)S(1)}, u32[]{:S(2)}, u32[]{:S(2)}) async-start(bf16[64,2,512]{2,1,0:T(2,128)(2,1)} %reshape.212), calls=%async_computation.1 | async-start | bytes 262144 | tf_op jit(solution)/shard_map/all_to_all | solution.py:28
  30.8 8.5 %all-to-all-done.1 = bf16[64,2,512]{2,1,0:T(2,128)(2,1)S(1)} async-done(((bf16[64,2,512]{2,1,0:T(2,128)(2,1)}), bf16[64,2,512]{2,1,0:T(2,128)(2,1)S(1)}, u32[]{:S(2)}, u32[]{:S(2)}) %all-to-all-start.1) | async-done | bytes 131104 | tf_op jit(solution)/shard_map/all_to_all | solution.py:28
  39.9 1.8 gather_fusion.1
  41.7 2.1 convolution_bitcast_fusion.1
  43.8 2.7 fusion.2
  49.1 4.4 %all-to-all-start.2 = ((bf16[64,2,512]{2,1,0:T(2,128)(2,1)}), bf16[64,2,512]{2,1,0:T(2,128)(2,1)S(1)}, u32[]{:S(2)}, u32[]{:S(2)}) async-start(bf16[64,2,512]{2,1,0:T(2,128)(2,1)} %reshape.214), calls=%async_computation.2 | async-start | bytes 262144 | tf_op jit(solution)/shard_map/all_to_all | solution.py:31
  54.3 10.6 %all-to-all-done.2 = bf16[64,2,512]{2,1,0:T(2,128)(2,1)S(1)} async-done(((bf16[64,2,512]{2,1,0:T(2,128)(2,1)}), bf16[64,2,512]{2,1,0:T(2,128)(2,1)S(1)}, u32[]{:S(2)}, u32[]{:S(2)}) %all-to-all-start.2) | async-done | bytes 131104 | tf_op jit(solution)/shard_map/all_to_all | solution.py:31
  64.9 10.0 %all-to-all-start = ((bf16[64,8,384]{2,0,1:T(8,128)(2,1)}), bf16[64,8,384]{2,0,1:T(8,128)(2,1)}, u32[]{:S(2)}, u32[]{:S(2)}) async-start(bf16[64,8,384]{2,0,1:T(8,128)(2,1)} %bitcast.123), calls=%async_computation | async-start | bytes 786432 | tf_op jit(solution)/shard_map/all_to_all | solution.py:65
  76.8 1.6 copy.79
  79.6 8.2 %scatter_custom_fusion = f32[64,3072]{0,1:T(8,128)} fusion(f32[64,3072]{0,1:T(8,128)} %copy.79, s32[1024]{0:T(1024)} %bitcast.145, bf16[64,1024]{0,1:T(8,128)(2,1)S(1)} %bitcast.138), kind=kCustom, calls=%fused_computation.41 | custom fusion | flops 131072 | bytes 917504 | tf_op jit(solution)/shard_map/scatter-add | solution.py:39
  90.3 6.6 %all-to-all-start.3 = ((bf16[64,8,384]{2,0,1:T(8,128)(2,1)}), bf16[64,8,384]{2,0,1:T(8,128)(2,1)}, u32[]{:S(2)}, u32[]{:S(2)}) async-start(bf16[64,8,384]{2,0,1:T(8,128)(2,1)} %copy.80), calls=%async_computation.3 | async-start | bytes 786432 | tf_op jit(solution)/shard_map/all_to_all | solution.py:66
  97.1 2.5 fusion.18
  99.6 10.7 %all-to-all-done.3 = bf16[64,8,384]{2,0,1:T(8,128)(2,1)} async-done(((bf16[64,8,384]{2,0,1:T(8,128)(2,1)}), bf16[64,8,384]{2,0,1:T(8,128)(2,1)}, u32[]{:S(2)}, u32[]{:S(2)}) %all-to-all-start.3) | async-done | bytes 393248 | tf_op jit(solution)/shard_map/all_to_all | solution.py:66
  110.4 3.0 %multiply_convert_fusion = (bf16[512,384]{1,0:T(8,128)(2,1)S(1)}, bf16[512,384]{1,0:T(8,128)(2,1)}) fusion(bf16[512,384]{1,0:T(8,128)(2,1)} %param.17, f32[512,384]{1,0:T(8,128)} %fusion.18, bf16[512,384]{1,0:T(8,128)(2,1)} %bitcast.19, bf16[2,512,512]{2,1,0:T(8,128)(2,1)} %param.12), kind=kOutput, calls=%fused_computation.29 | convolution fusion | flops 203882496 | bytes 2883584 | tf_op jit(solution)/shard_map/io,iv->ov/dot_general | solution.py:69
  113.7 73.1 %all_to_all.85 = bf16[8,512,384]{2,1,0:T(8,128)(2,1)S(1)} all-to-all(bf16[8,512,384]{2,1,0:T(8,128)(2,1)S(1)} %stack.8), channel_id=1, replica_groups=mesh['dom'=64,'feat'=8] {'feat'}, dimensions={0} | all-to-all | bytes 6291456 | tf_op jit(solution)/shard_map/all_to_all | solution.py:78
  191.3 5.5 %copy.82 = bf16[512,8,384]{2,1,0:T(8,128)(2,1)} copy(bf16[512,8,384]{2,0,1:T(8,128)(2,1)} %bitcast.126) | data formatting | bytes 6291456 | tf_op jit(solution)/shard_map/reshape | solution.py:77
  196.8 5.8 %reshape.205 = bf16[512,3072,1]{1,0,2:T(8,128)(2,1)} reshape(bf16[512,8,384]{2,1,0:T(8,128)(2,1)} %copy.82) | data formatting | bytes 6291456 | tf_op jit(solution)/shard_map/reshape | solution.py:77
  202.7 2.5 convolution_convert_fusion
  206.5 4.3 %gather_fusion.2 = bf16[1024,64]{1,0:T(8,128)(2,1)} fusion(bf16[64,3072]{0,1:T(8,128)(2,1)S(1)} %copy.83, s32[1024]{0:T(1024)S(1)} %fusion.33), kind=kCustom, calls=%fused_computation.2.clone | custom fusion | bytes 266240 | tf_op jit(solution)/shard_map/jit(_take)/gather | solution.py:25
  212.3 18.4 %all_to_all.86 = bf16[64,2,512]{2,1,0:T(2,128)(2,1)S(1)} all-to-all(bf16[64,2,512]{2,1,0:T(2,128)(2,1)S(1)} %reshape.216), channel_id=1, replica_groups=mesh['dom'=64,'feat'=8] {'dom'}, dimensions={0} | all-to-all | bytes 262144 | tf_op jit(solution)/shard_map/all_to_all | solution.py:28
  231.2 1.9 gather_fusion.3
  233.1 3.0 %convolution_bitcast_fusion = f32[64,72,128]{2,0,1:T(8,128)S(1)} fusion(bf16[72,128,128]{2,1,0:T(8,128)(2,1)S(1)} %copy-done, bf16[72,64,128]{2,1,0:T(8,128)(2,1)} %gather_fusion.3, pred[72]{0:T(512)(128)(4,1)S(1)} %copy-done.11), kind=kOutput, calls=%fused_computation.12 | convolution fusion | flops 151584768 | bytes 5898312 | tf_op jit(solution)/shard_map/ftd,tsd->fts/dot_general | solution.py:53
  236.1 2.7 fusion
  240.3 1.8 reshape.218
  242.0 4.4 %all-to-all-start.6 = ((bf16[64,2,512]{2,1,0:T(2,128)(2,1)}), bf16[64,2,512]{2,1,0:T(2,128)(2,1)S(1)}, u32[]{:S(2)}, u32[]{:S(2)}) async-start(bf16[64,2,512]{2,1,0:T(2,128)(2,1)} %reshape.218), calls=%async_computation.6 | async-start | bytes 262144 | tf_op jit(solution)/shard_map/all_to_all | solution.py:31
  246.5 2.0 slice_add_fusion
  248.5 2.8 copy.88
  251.3 7.4 %all-to-all-done.6 = bf16[64,2,512]{2,1,0:T(2,128)(2,1)S(1)} async-done(((bf16[64,2,512]{2,1,0:T(2,128)(2,1)}), bf16[64,2,512]{2,1,0:T(2,128)(2,1)S(1)}, u32[]{:S(2)}, u32[]{:S(2)}) %all-to-all-start.6) | async-done | bytes 131104 | tf_op jit(solution)/shard_map/all_to_all | solution.py:31
  258.9 8.2 %scatter_custom_fusion.1 = f32[64,3072]{0,1:T(8,128)} fusion(f32[64,3072]{0,1:T(8,128)} %copy.88, s32[1024]{0:T(1024)} %bitcast.146, bf16[64,1024]{0,1:T(8,128)(2,1)S(1)} %bitcast.137), kind=kCustom, calls=%fused_computation.39 | custom fusion | flops 131072 | bytes 917504 | tf_op jit(solution)/shard_map/scatter-add | solution.py:39
  269.7 5.5 %all-gather.2.cloned.1.call-done = bf16[64,2,64,512]{3,2,1,0:T(8,128)(2,1)} async-done(((bf16[1,2,64,512]{3,2,1,0:T(8,128)(2,1)}), bf16[64,2,64,512]{3,2,1,0:T(8,128)(2,1)}) %all-gather.2.cloned.1.call-update) | async-done | bytes 8388624 | tf_op jit(solution)/shard_map/all_gather | solution.py:8
  275.2 5.5 %convert_reduce_fusion = f32[2,64,512]{2,1,0:T(8,128)} fusion(bf16[64,2,64,512]{3,2,1,0:T(8,128)(2,1)} %all-gather.2.cloned.1.call-done), kind=kLoop, calls=%fused_computation.6 | loop fusion | flops 8323072 | bytes 8650752 | tf_op jit(solution)/shard_map/reduce_sum | solution.py:9
  (72 shorter events, 28.9 us)
Async XLA Ops:
  7.2 34.5 %copy-start = (bf16[72,128,128]{2,1,0:T(8,128)(2,1)S(1)}, bf16[72,128,128]{2,1,0:T(8,128)(2,1)}, u32[]{:S(2)}) copy-start(bf16[72,128,128]{2,1,0:T(8,128)(2,1)} %param.13) | copy-start | bytes 7077892
  7.2 32.5 %copy-start.2 = (bf16[64,3072]{1,0:T(8,128)(2,1)S(1)}, bf16[64,3072]{1,0:T(8,128)(2,1)}, u32[]{:S(2)}) copy-start(bf16[64,3072]{1,0:T(8,128)(2,1)} %param.11) | copy-start | bytes 1179652
  7.2 21.0 %copy-start.8 = (s32[72,2]{0,1:T(2,128)S(1)}, s32[72,2]{0,1:T(2,128)}, u32[]{:S(2)}) copy-start(s32[72,2]{0,1:T(2,128)} %param.14) | copy-start | bytes 1732
  8.1 0.6 copy-start.6
  16.6 22.7 %all-to-all-start.1 = ((bf16[64,2,512]{2,1,0:T(2,128)(2,1)}), bf16[64,2,512]{2,1,0:T(2,128)(2,1)S(1)}, u32[]{:S(2)}, u32[]{:S(2)}) async-start(bf16[64,2,512]{2,1,0:T(2,128)(2,1)} %reshape.212), calls=%async_computation.1 | async-start | bytes 262144 | tf_op jit(solution)/shard_map/all_to_all | solution.py:28
  29.5 14.3 %copy-start.9 = (f32[72]{0:T(128)}, f32[72]{0:T(128)S(1)}, u32[]{:S(2)}) copy-start(f32[72]{0:T(128)S(1)} %compare_convert_fusion) | copy-start | bytes 868
  46.4 28.5 %copy-start.7 = (s32[1,64,16]{2,1,0:T(8,128)S(1)}, s32[1,64,16]{2,1,0:T(8,128)}, u32[]{:S(2)}) copy-start(s32[1,64,16]{2,1,0:T(8,128)} %copy-done.6) | copy-start | bytes 12292
  47.0 1.0 copy-start.3
  49.1 15.8 %all-to-all-start.2 = ((bf16[64,2,512]{2,1,0:T(2,128)(2,1)}), bf16[64,2,512]{2,1,0:T(2,128)(2,1)S(1)}, u32[]{:S(2)}, u32[]{:S(2)}) async-start(bf16[64,2,512]{2,1,0:T(2,128)(2,1)} %reshape.214), calls=%async_computation.2 | async-start | bytes 262144 | tf_op jit(solution)/shard_map/all_to_all | solution.py:31
  64.9 10.1 %copy-start.5 = (bf16[64,2,512]{2,1,0:T(2,128)(2,1)}, bf16[64,2,512]{2,1,0:T(2,128)(2,1)S(1)}, u32[]{:S(2)}) copy-start(bf16[64,2,512]{2,1,0:T(2,128)(2,1)S(1)} %all-to-all-done.2) | copy-start | bytes 393220
  64.9 25.4 %all-to-all-start = ((bf16[64,8,384]{2,0,1:T(8,128)(2,1)}), bf16[64,8,384]{2,0,1:T(8,128)(2,1)}, u32[]{:S(2)}, u32[]{:S(2)}) async-start(bf16[64,8,384]{2,0,1:T(8,128)(2,1)} %bitcast.123), calls=%async_computation | async-start | bytes 786432 | tf_op jit(solution)/shard_map/all_to_all | solution.py:65
  90.3 20.1 %all-to-all-start.3 = ((bf16[64,8,384]{2,0,1:T(8,128)(2,1)}), bf16[64,8,384]{2,0,1:T(8,128)(2,1)}, u32[]{:S(2)}, u32[]{:S(2)}) async-start(bf16[64,8,384]{2,0,1:T(8,128)(2,1)} %copy.80), calls=%async_computation.3 | async-start | bytes 786432 | tf_op jit(solution)/shard_map/all_to_all | solution.py:66
  96.9 178.3 %all-gather.2.cloned.1.call-start = ((), (), s32[]{:S(2)}) async-start(), calls=%async_computation.7 | async-start | bytes 8519680 | tf_op jit(solution)/shard_map/all_gather | solution.py:8
  186.8 1.7 copy-start.1
  205.2 0.9 copy-start.4
  212.1 21.0 %copy-start.11 = (pred[72]{0:T(512)(128)(4,1)S(1)}, pred[72]{0:T(512)(128)(4,1)}, u32[]{:S(2)}) copy-start(pred[72]{0:T(512)(128)(4,1)} %get-tuple-element.20) | copy-start | bytes 220
  233.1 3.0 %copy-start.10 = (f32[72]{0:T(128)S(1)}, f32[72]{0:T(128)}, u32[]{:S(2)}) copy-start(f32[72]{0:T(128)} %copy-done.9) | copy-start | bytes 868
  233.1 3.0 %copy-start.12 = (s32[72]{0:T(128)S(1)}, s32[72]{0:T(128)}, u32[]{:S(2)}) copy-start(s32[72]{0:T(128)} %get-tuple-element.28) | copy-start | bytes 868
  242.0 16.7 %all-to-all-start.6 = ((bf16[64,2,512]{2,1,0:T(2,128)(2,1)}), bf16[64,2,512]{2,1,0:T(2,128)(2,1)S(1)}, u32[]{:S(2)}, u32[]{:S(2)}) async-start(bf16[64,2,512]{2,1,0:T(2,128)(2,1)} %reshape.218), calls=%async_computation.6 | async-start | bytes 262144 | tf_op jit(solution)/shard_map/all_to_all | solution.py:31
Sparse Core Ops, SparseCore 0:
  191.5 83.6 all-gather.1
